TPU v7x, 32 devices: a whole 2x2x4 slice. The times are simulated.
32 devices in a mesh: grp: 1, seq: 32 (over z, y, x, core).
Axes of the slice: x: 2, y: 2, z: 4, core: 2. Of those that a mesh axis runs over, the one named last changes fastest.
Arguments:
- tokens: bfloat16 [4096, 4096], P(('grp', 'seq')), may hold values from -6 to 6
- gain: float32 [4096], replicated, may hold values from 0.5 to 6, as said below
- w_query: bfloat16 [4096, 2048], P('seq'), may hold values from -0.09375 to 0.09375
- key_value_weight: bfloat16 [4096, 1024], P('seq'), may hold values from -0.09375 to 0.09375
Outputs:
- attended: bfloat16 [4096, 2048], P(('grp', 'seq'))
Inputs may be any that keep to these rules, and one draw needn't show every extreme that they name: gain is the same for all groups.
All inputs are finite; a program needn't handle non-finite values.
Results may differ from a plain program's by a relative error of at most 0.0055.
The roundings to bfloat16 on the way count: a program that leaves them out, or rounds other values in their place, can miss the bound.
Values may be sent and summed in bfloat16 or wider, within the bound.
A program may use at most 128 MiB of HBM per device.

v0:
```python
import math

import jax
import jax.numpy as jnp
from jax import lax
from jax.sharding import PartitionSpec as P

HEAD_WIDTH = 128
HQ = 16


ROPE_BASE = 500000.0


def apply_rotation(heads_in, token_positions):
    half_dim = HEAD_WIDTH // 2
    frequency = ROPE_BASE ** (-(jnp.arange(half_dim, dtype=jnp.float32) * 2.0 / HEAD_WIDTH))
    angles = token_positions.astype(jnp.float32)[:, None] * frequency[None, :]
    cosine = jnp.cos(angles)[:, None, :]
    sine_part = jnp.sin(angles)[:, None, :]
    first = heads_in[..., :half_dim]
    second = heads_in[..., half_dim:]
    return jnp.concatenate(
        [first * cosine - second * sine_part, second * cosine + first * sine_part], axis=-1
    )


def attend_block(state, query_part, kv_block, key_start, own_index, tok_rows):
    run_max, totals, weighted = state
    scale = 1.0 / HEAD_WIDTH**0.5
    key_count = kv_block.shape[1]
    scores = (
        jnp.einsum("qhgd,khd->qhgk", query_part, kv_block[0], preferred_element_type=jnp.float32)
        * scale
    )
    query_pos = own_index * tok_rows + jnp.arange(tok_rows, dtype=jnp.int32)
    key_pos = key_start + jnp.arange(key_count, dtype=jnp.int32)
    allowed = key_pos[None, :] <= query_pos[:, None]
    scores = jnp.where(allowed[:, None, None, :], scores, -1e30)
    new_max = jnp.maximum(run_max, jnp.max(scores, axis=-1))
    shrink = jnp.exp(run_max - new_max)
    expo = jnp.exp(scores - new_max[..., None])
    totals = totals * shrink + jnp.sum(expo, axis=-1)
    update = jnp.einsum(
        "qhgk,khd->qhgd", expo.astype(jnp.bfloat16), kv_block[1], preferred_element_type=jnp.float32
    )
    weighted = weighted * shrink[..., None] + update
    return (new_max, totals, weighted)


def fresh_state(tok_rows, kv_heads, group_size):
    return (
        jnp.full((tok_rows, kv_heads, group_size), -1e30, jnp.float32),
        jnp.zeros((tok_rows, kv_heads, group_size), jnp.float32),
        jnp.zeros((tok_rows, kv_heads, group_size, HEAD_WIDTH), jnp.float32),
    )


def on_device(tokens, gain, w_query, key_value_weight):
    tok_rows = tokens.shape[0]
    tok_float = tokens.astype(jnp.float32)
    mean_sq = jnp.mean(tok_float * tok_float, axis=-1, keepdims=True)
    normed = (tok_float * lax.rsqrt(mean_sq + 1e-05) * gain[None, :]).astype(jnp.bfloat16)

    def add_rows(weight_piece):
        return jnp.dot(normed, weight_piece, preferred_element_type=jnp.float32)

    query_raw = add_rows(lax.all_gather(w_query, "seq", axis=0, tiled=True))
    key_value_rows = add_rows(lax.all_gather(key_value_weight, "seq", axis=0, tiled=True))
    kv_heads = key_value_weight.shape[1] // (2 * HEAD_WIDTH)
    group_size = HQ // kv_heads
    own_index = lax.axis_index("seq")
    token_positions = own_index * tok_rows + jnp.arange(tok_rows, dtype=jnp.int32)
    query_matrix = apply_rotation(
        query_raw.reshape(tok_rows, HQ, HEAD_WIDTH), token_positions
    ).astype(jnp.bfloat16)
    query_matrix = query_matrix.reshape(tok_rows, kv_heads, group_size, HEAD_WIDTH)
    key_head_rows = apply_rotation(
        key_value_rows[:, : kv_heads * HEAD_WIDTH].reshape(tok_rows, kv_heads, HEAD_WIDTH),
        token_positions,
    ).astype(jnp.bfloat16)
    value_head_rows = (
        key_value_rows[:, kv_heads * HEAD_WIDTH :]
        .reshape(tok_rows, kv_heads, HEAD_WIDTH)
        .astype(jnp.bfloat16)
    )
    kv_local = jnp.stack([key_head_rows, value_head_rows])
    piece = lax.all_gather(kv_local, "seq", axis=1, tiled=True)
    piece_len = piece.shape[1]
    block_len = math.gcd(tok_rows, piece_len)
    block_count = piece_len // block_len

    def inner(block_index, held):
        block = lax.dynamic_slice_in_dim(piece, block_index * block_len, block_len, 1)
        return attend_block(held, query_matrix, block, block_index * block_len, own_index, tok_rows)

    final = lax.fori_loop(0, block_count, inner, fresh_state(tok_rows, kv_heads, group_size))
    totals = final[1]
    weighted = final[2]
    result = weighted / totals[..., None]
    return result.reshape(tok_rows, HQ * HEAD_WIDTH).astype(jnp.bfloat16)


def solution(mesh):
    return jax.shard_map(
        on_device,
        mesh=mesh,
        in_specs=(P(("grp", "seq"), None), P(), P("seq", None), P("seq", None)),
        out_specs=P(("grp", "seq"), None),
        check_vma=False,
    )
```

profile of v0, /device:TPU:27, one launch (start us, length us, event | category | flops | bytes accessed | tf_op | source)
XLA Modules:
  0.0 384.3 jit_solution(3070043374559570994)
XLA Ops:
  8.1 1.5 fusion.10
  10.0 77.7 %all-gather.4.cloned.1.call-done = bf16[4096,1024]{1,0:T(8,128)(2,1)} async-done(((bf16[128,1024]{1,0:T(8,128)(2,1)}), bf16[4096,1024]{1,0:T(8,128)(2,1)}) %all-gather.4.cloned.1.call-update) | async-done | bytes 8388624 | tf_op jit(solution)/shard_map/all_gather | solution.py:69
  87.6 5.0 %fusion.14 = f32[128,1024]{1,0:T(8,128)S(1)} fusion(bf16[4096,1024]{1,0:T(8,128)(2,1)} %all-gather.4.cloned.1.call-done, bf16[128,4096]{1,0:T(8,128)(2,1)} %param.6, f32[4096]{0:T(1024)} %param.7, f32[128]{0:T(128)S(1)} %add_rsqrt_fusion), kind=kOutput, calls=%fused_computation.31 | convolution fusion | flops 1075838976 | bytes 9978368 | tf_op jit(solution)/shard_map/dot_general | solution.py:66
  94.0 109.3 %all-gather.8.cloned.1.call-done = bf16[4096,2048]{1,0:T(8,128)(2,1)} async-done(((bf16[128,2048]{1,0:T(8,128)(2,1)}), bf16[4096,2048]{1,0:T(8,128)(2,1)}) %all-gather.8.cloned.1.call-update) | async-done | bytes 16777232 | tf_op jit(solution)/shard_map/all_gather | solution.py:68
  203.3 8.1 %convolution_bitcast_fusion.1 = f32[16,8,16,128]{3,1,2,0:T(8,128)S(1)} fusion(bf16[4096,2048]{1,0:T(8,128)(2,1)} %all-gather.8.cloned.1.call-done, bf16[128,4096]{1,0:T(8,128)(2,1)S(1)} %copy-done, f32[4096]{0:T(1024)S(1)} %copy-done.1, f32[128]{0:T(128)S(1)} %add_rsqrt_fusion), kind=kOutput, calls=%fused_computation.26 | convolution fusion | flops 2149580800 | bytes 18891264 | tf_op jit(solution)/shard_map/dot_general | solution.py:66
  212.8 69.2 %all-gather.6.cloned.1.call-done = bf16[2,4096,4,128]{3,1,2,0:T(8,128)(2,1)} async-done(((bf16[2,128,4,128]{3,1,2,0:T(8,128)(2,1)}), bf16[2,4096,4,128]{3,1,2,0:T(8,128)(2,1)}) %all-gather.6.cloned.1.call-update) | async-done | bytes 8388624 | tf_op jit(solution)/shard_map/all_gather | solution.py:88
  282.0 94.6 %while.20 = (s32[]{:T(128)}, f32[128,4,4]{0,2,1:T(4,128)S(1)}, f32[128,4,4]{0,2,1:T(4,128)S(1)}, f32[128,4,4,128]{0,3,2,1:T(8,128)S(1)}, s32[]{:T(128)}, /*index...) while((s32[]{:T(128)}, f32[128,4,4]{0,2,1:T(4,128)S(1)}, ...), condition=%wide.region_4.5_spmd.clone, body=%wide.region_1.4_spmd.clone.sunk | while | flops 136866048 | bytes 6195415 | solution.py:97
  282.1 1.2 fusion.31
  283.5 1.4 fusion.34
  286.5 1.4 fusion.34
  289.4 1.4 fusion.34
  292.4 1.4 fusion.34
  293.9 1.2 fusion.31
  295.3 1.4 fusion.34
  296.8 1.2 fusion.31
  298.3 1.4 fusion.34
  301.3 1.4 fusion.34
  304.2 1.4 fusion.34
  307.2 1.4 fusion.34
  310.1 1.4 fusion.34
  313.1 1.4 fusion.34
  314.6 1.2 fusion.31
  316.0 1.4 fusion.34
  319.0 1.4 fusion.34
  322.0 1.4 fusion.34
  324.9 1.4 fusion.34
  327.9 1.4 fusion.34
  329.4 1.2 fusion.31
  330.8 1.4 fusion.34
  332.3 1.2 fusion.31
  333.8 1.4 fusion.34
  336.7 1.4 fusion.34
  339.7 1.4 fusion.34
  342.7 1.4 fusion.34
  345.6 1.4 fusion.34
  347.1 1.2 fusion.31
  348.6 1.4 fusion.34
  350.1 1.2 fusion.31
  351.5 1.4 fusion.34
  354.5 1.4 fusion.34
  357.4 1.4 fusion.34
  360.4 1.4 fusion.34
  363.4 1.4 fusion.34
  366.3 1.4 fusion.34
  367.8 1.2 fusion.31
  369.3 1.4 fusion.34
  372.2 1.4 fusion.34
  375.2 1.4 fusion.34
  (247 shorter events, 43.2 us)
Async XLA Ops:
  6.5 81.1 %all-gather.4.cloned.1.call-start = ((), (), s32[]{:S(2)}) async-start(), calls=%async_computation | async-start | bytes 8650752 | tf_op jit(solution)/shard_map/all_gather | solution.py:69
  7.3 196.0 %all-gather.8.cloned.1.call-start = ((), (), s32[]{:S(2)}) async-start(), calls=%async_computation.2 | async-start | bytes 17301504 | tf_op jit(solution)/shard_map/all_gather | solution.py:68
  8.0 274.0 %all-gather.6.cloned.1.call-start = ((), (), s32[]{:S(2)}) async-start(), calls=%async_computation.1 | async-start | bytes 8650752 | tf_op jit(solution)/shard_map/all_gather | solution.py:88
  9.9 193.4 %copy-start = (bf16[128,4096]{1,0:T(8,128)(2,1)S(1)}, bf16[128,4096]{1,0:T(8,128)(2,1)}, u32[]{:S(2)}) copy-start(bf16[128,4096]{1,0:T(8,128)(2,1)} %param.6) | copy-start | bytes 3145732
  9.9 193.4 %copy-start.1 = (f32[4096]{0:T(1024)S(1)}, f32[4096]{0:T(1024)}, u32[]{:S(2)}) copy-start(f32[4096]{0:T(1024)} %param.7) | copy-start | bytes 49156
Sparse Core Ops, SparseCore 0:
  10.2 77.3 all-gather.3
  90.5 112.7 all-gather.7
  206.2 75.6 all-gather.5
where the time goes:
time: 389 us; the launch traced here: 384 us
  waiting for transfers between devices  258 us (66%)
  matrix products  96.2 us (25%)
  between operations  13.3 us (3%)
  other arithmetic  12.9 us (3%)
    all_gather x1, waiting for transfers between devices, on_device(): query_raw = add_rows(lax.all_gather(w_query, 'seq', axis=0, tiled=True))  109 us
    all_gather x1, waiting for transfers between devices, on_device(): lax.all_gather(key_value_weight, 'seq', axis=0, tiled=True)  77.7 us
    all_gather x1, waiting for transfers between devices, on_device(): piece = lax.all_gather(kv_local, 'seq', axis=1, tiled=True)  69.2 us
    dot_general x32, matrix products, attend_block(): jnp.einsum('qhgk,khd->qhgd', expo.astype(jnp.bfloat16), kv_block[1], pref...  43.6 us
    dot_general x32, matrix products, attend_block(): jnp.einsum('qhgd,khd->qhgk', query_part, kv_block[0], preferred_element_t...  39.5 us
    dot_general x2, matrix products, add_rows(): return jnp.dot(normed, weight_piece, preferred_element_type=jnp.float32)  13.2 us
  transfers between devices with their start and end apart: 3, of which 3 were waited for; matrix products, arithmetic and copies ran while one was open for 5% of the time, Pallas kernels for 0%

commit v1 on v0

v1 whole, which is shorter than its diff:
```python
import functools

import jax
import jax.numpy as jnp
from jax import lax
from jax.experimental import pallas as pl
from jax.experimental.pallas import tpu as pltpu
from jax.sharding import PartitionSpec as P

HEAD_WIDTH = 128
HQ = 16
ROPE_BASE = 500000.0
LOG2E = 1.4426950408889634
MESH = pl.DeviceIdType.MESH


def kernel(
    planes, kv_heads, tok_ref, gain_ref, wq_ref, wkv_ref, cos_ref, sin_ref, out_ref,
    wst, wbuf, xbuf, acc, qbuf, kvbuf, mbuf, lbuf, obuf, ost, orecv,
    ws, wr, xs, xr, us, ur, ds_, dr, ss, sr, ks, kr, kss, ksr, os_, orr,
):
    C, Z, D = kv_heads, planes, HEAD_WIDTH
    T, M = tok_ref.shape
    G = HQ // C
    QW = G * D
    R = C * T
    me = lax.axis_index("seq")
    z = me // (2 * C)
    p = (me % (2 * C)) // 2
    k = me % 2

    def dev(zi, pi, ki):
        return {"seq": (zi * C + pi) * 2 + ki}

    sibling = dev(z, p, 1 - k)
    above = dev(lax.rem(z + 1, Z), p, k)
    below = dev(lax.rem(z + Z - 1, Z), p, k)
    has_above = z < Z - 1
    has_below = z > 0

    def copy(src, dst, send, recv, device):
        return pltpu.make_async_remote_copy(
            src_ref=src, dst_ref=dst, send_sem=send, recv_sem=recv,
            device_id=device, device_id_type=MESH,
        )

    barrier = pltpu.get_barrier_semaphore()
    for d in range(1, C):
        pl.semaphore_signal(barrier, inc=1, device_id=dev(z, lax.rem(p + d, C), k), device_id_type=MESH)
    pl.semaphore_signal(barrier, inc=1, device_id=sibling, device_id_type=MESH)

    @pl.when(has_above)
    def _():
        pl.semaphore_signal(barrier, inc=1, device_id=above, device_id_type=MESH)

    @pl.when(has_below)
    def _():
        pl.semaphore_signal(barrier, inc=1, device_id=below, device_id_type=MESH)

    for c in range(C):
        wst[c, :, :QW] = wq_ref[:, c * QW:(c + 1) * QW]
        wst[c, :, QW:QW + D] = wkv_ref[:, c * D:(c + 1) * D]
        wst[c, :, QW + D:] = wkv_ref[:, (C + c) * D:(C + c + 1) * D]
    mine = pl.ds(pl.multiple_of(p * T, T), T)
    wbuf[z, k, mine, :] = wst[p]

    pl.semaphore_wait(barrier, C + has_above.astype(jnp.int32) + has_below.astype(jnp.int32))

    def w_copy(d):
        to = lax.rem(p + d, C)
        return copy(wst.at[to], wbuf.at[z, k, mine, :], ws.at[d], wr.at[d], dev(z, to, k))

    def x_copy(d):
        part = xbuf.at[:, mine, :]
        return copy(part, part, xs.at[d], xr.at[d], dev(z, lax.rem(p + d, C), k))

    for d in range(1, C):
        w_copy(d).start()

    @pl.loop(0, T // 16)
    def _(i):
        x = tok_ref[pl.ds(pl.multiple_of(i * 16, 16), 16), :].astype(jnp.float32)
        mean_sq = jnp.mean(x * x, axis=-1, keepdims=True)
        y = (x * lax.rsqrt(mean_sq + 1e-05) * gain_ref[...]).astype(jnp.bfloat16)
        rows = pl.ds(pl.multiple_of(p * T + i * 16, 16), 16)
        for zi in range(Z):
            for ki in range(2):
                for c in range(C):
                    j = ((zi * C + c) * 2 + ki) * T
                    xbuf[zi * 2 + ki, rows, c * T:(c + 1) * T] = y[:, j:j + T]

    for d in range(1, C):
        x_copy(d).start()

    def w_recv(d):
        frm = lax.rem(p + C - d, C)
        slot = wbuf.at[z, k, pl.ds(pl.multiple_of(frm * T, T), T), :]
        copy(slot, slot, ws.at[d], wr.at[d], sibling).wait_recv()

    def x_recv(d):
        frm = lax.rem(p + C - d, C)
        slot = xbuf.at[:, pl.ds(pl.multiple_of(frm * T, T), T), :]
        copy(slot, slot, xs.at[d], xr.at[d], sibling).wait_recv()

    def block_copy(buf, zi, ki, send, recv, device):
        slot = buf.at[zi, ki]
        return copy(slot, slot, send, recv, device)

    def plane_of(zi):
        return lax.rem(zi + Z, Z)

    def up(t):
        return block_copy(wbuf, plane_of(z - t), k, us.at[t], ur.at[t], above)

    def down(t):
        return block_copy(wbuf, plane_of(z + t), k, ds_.at[t], dr.at[t], below)

    def sib(index, zi, ki):
        return block_copy(wbuf, zi, ki, ss.at[index], sr.at[index], sibling)

    for d in range(1, C):
        w_recv(d)

    @pl.when(has_above)
    def _():
        up(0).start()

    @pl.when(has_below)
    def _():
        down(0).start()

    sib(0, z, k).start()

    def step(t):
        @pl.when(z >= t)
        def _():
            block_copy(wbuf, plane_of(z - t), k, us.at[t - 1], ur.at[t - 1], below).wait_recv()

            @pl.when(has_above)
            def _():
                up(t).start()

            sib(t, plane_of(z - t), k).start()

        @pl.when(z + t < Z)
        def _():
            block_copy(wbuf, plane_of(z + t), k, ds_.at[t - 1], dr.at[t - 1], above).wait_recv()

            @pl.when(has_below)
            def _():
                down(t).start()

            sib(Z - 1 + t, plane_of(z + t), k).start()

    def project(zi, index):
        sib(index, zi, 1 - k).wait_recv()

        @pl.loop(0, R // 256)
        def _(i):
            rows = pl.ds(pl.multiple_of(i * 256, 256), 256)
            total = acc[rows, :]
            for ki in range(2):
                total += jnp.dot(
                    xbuf[zi * 2 + ki, rows, :], wbuf[zi, ki],
                    preferred_element_type=jnp.float32,
                )
            acc[rows, :] = total

    def project_step(t):
        @pl.when(z >= t)
        def _():
            project(plane_of(z - t), t)

        @pl.when(z + t < Z)
        def _():
            project(plane_of(z + t), Z - 1 + t)

    acc[...] = jnp.zeros_like(acc)
    for t in range(1, Z - 1):
        step(t)
    for d in range(1, C):
        x_recv(d)
    project(z, 0)
    for t in range(1, Z - 1):
        project_step(t)
    if Z > 1:
        step(Z - 1)
        project_step(Z - 1)

    cos, sin = cos_ref[...], sin_ref[...]

    def rope(u):
        return (u * cos + pltpu.roll(u, D // 2, 1) * sin).astype(jnp.bfloat16)

    kvbuf[z, k, :, :D] = rope(acc[:, QW:QW + D])
    kvbuf[z, k, :, D:] = acc[:, QW + D:].astype(jnp.bfloat16)

    def kv_up(t):
        return block_copy(kvbuf, plane_of(z - t), k, ks.at[t], kr.at[t], above)

    def kv_sib(t, ki):
        return block_copy(kvbuf, plane_of(z - t), ki, kss.at[t], ksr.at[t], sibling)

    kv_sib(0, k).start()

    @pl.when(has_above)
    def _():
        kv_up(0).start()

    for h in range(G):
        qbuf[h] = rope(acc[:, h * D:(h + 1) * D])

    factor = LOG2E / D**0.5
    half = R // 256

    def attend(zi, first):
        @pl.loop(0, G * half)
        def _(i):
            h = i // half
            r0 = pl.multiple_of((i % half) * 256, 256)
            rows = pl.ds(r0, 256)
            q = qbuf[h, rows, :]
            keys = kvbuf[zi, :, :, :D].reshape(2 * R, D)
            vals = kvbuf[zi, :, :, D:].reshape(2 * R, D)
            s = lax.dot_general(
                q, keys, (((1,), (1,)), ((), ())), preferred_element_type=jnp.float32
            )
            if first:
                row = r0 + lax.broadcasted_iota(jnp.int32, (256, 1), 0)
                col = lax.broadcasted_iota(jnp.int32, (1, 2 * R), 1)
                qpos = ((row // T) * 2 + k) * T + row % T
                kpos = (((col % R) // T) * 2 + col // R) * T + col % T
                s = jnp.where(kpos <= qpos, s, -1e30)
                m = jnp.max(s, axis=-1, keepdims=True)
            else:
                old = mbuf[h, rows, :1]
                m = jnp.maximum(old, jnp.max(s, axis=-1, keepdims=True))
            e = jnp.exp2((s - m) * factor)
            total = jnp.sum(e, axis=-1, keepdims=True)
            o = jnp.dot(e.astype(jnp.bfloat16), vals, preferred_element_type=jnp.float32)
            if not first:
                shrink = jnp.exp2((old - m) * factor)
                total += lbuf[h, rows, :1] * shrink
                o += obuf[h, rows, :] * shrink
            mbuf[h, rows, :] = jnp.broadcast_to(m, (256, D))
            lbuf[h, rows, :] = jnp.broadcast_to(total, (256, D))
            obuf[h, rows, :] = o

    def kv_recv(t):
        @pl.when(z >= t)
        def _():
            block_copy(kvbuf, plane_of(z - t), k, ks.at[t - 1], kr.at[t - 1], below).wait_recv()

            @pl.when(has_above)
            def _():
                kv_up(t).start()

            kv_sib(t, k).start()

    kv_sib(0, 1 - k).wait_recv()
    attend(z, True)
    for t in range(1, Z):
        kv_recv(t)

        @pl.when(z >= t)
        def _():
            kv_sib(t, 1 - k).wait_recv()
            attend(plane_of(z - t), False)

    for c in range(C):
        for h in range(G):
            ost[c, :, h * D:(h + 1) * D] = (
                obuf[h, c * T:(c + 1) * T, :] / lbuf[h, c * T:(c + 1) * T, :]
            ).astype(jnp.bfloat16)

    def o_copy(d):
        to = lax.rem(p + d, C)
        return copy(ost.at[to], orecv.at[p], os_.at[d], orr.at[d], dev(z, to, k))

    for d in range(1, C):
        o_copy(d).start()
    orecv[p] = ost[p]
    for d in range(1, C):
        frm = lax.rem(p + C - d, C)
        copy(orecv.at[frm], orecv.at[frm], os_.at[d], orr.at[d], sibling).wait_recv()
    for c in range(C):
        out_ref[:, c * QW:(c + 1) * QW] = orecv[c]

    for d in range(1, C):
        w_copy(d).wait_send()
        x_copy(d).wait_send()
        o_copy(d).wait_send()
    for t in range(Z):
        @pl.when(jnp.logical_and(has_above, z >= t))
        def _():
            up(t).wait_send()
            kv_up(t).wait_send()

        @pl.when(jnp.logical_and(has_below, z + t < Z))
        def _():
            down(t).wait_send()

        @pl.when(z >= t)
        def _():
            sib(t, plane_of(z - t), k).wait_send()
            kv_sib(t, k).wait_send()

        if t > 0:
            @pl.when(z + t < Z)
            def _():
                sib(Z - 1 + t, plane_of(z + t), k).wait_send()


def on_device(planes, tokens, gain, w_query, key_value_weight):
    T, M = tokens.shape
    D = HEAD_WIDTH
    C = key_value_weight.shape[1] // (2 * D)
    G = HQ // C
    R = C * T
    Z = planes
    width = (G + 2) * D
    me = lax.axis_index("seq")
    first = (me // (2 * C)) * (2 * C) + me % 2
    row = jnp.arange(R, dtype=jnp.int32)
    positions = (first + (row // T) * 2) * T + row % T
    lane = jnp.arange(D, dtype=jnp.int32)
    half = (lane % (D // 2)).astype(jnp.float32)
    frequency = ROPE_BASE ** (-(half * 2.0 / D))
    angles = positions.astype(jnp.float32)[:, None] * frequency[None, :]
    cos = jnp.cos(angles)
    sin = jnp.where(lane < D // 2, -1.0, 1.0)[None, :] * jnp.sin(angles)
    bf, f32 = jnp.bfloat16, jnp.float32
    sem = pltpu.SemaphoreType.DMA
    vm = pl.BlockSpec(memory_space=pltpu.VMEM)
    return pl.pallas_call(
        functools.partial(kernel, Z, C),
        out_shape=jax.ShapeDtypeStruct((T, HQ * D), bf),
        in_specs=[vm] * 6,
        out_specs=vm,
        scratch_shapes=[
            pltpu.VMEM((C, T, width), bf),
            pltpu.VMEM((Z, 2, R, width), bf),
            pltpu.VMEM((2 * Z, R, M // (2 * Z)), bf),
            pltpu.VMEM((R, width), f32),
            pltpu.VMEM((G, R, D), bf),
            pltpu.VMEM((Z, 2, R, 2 * D), bf),
            pltpu.VMEM((G, R, D), f32),
            pltpu.VMEM((G, R, D), f32),
            pltpu.VMEM((G, R, D), f32),
            pltpu.VMEM((C, T, G * D), bf),
            pltpu.VMEM((C, T, G * D), bf),
            sem((C,)), sem((C,)), sem((C,)), sem((C,)),
            sem((Z,)), sem((Z,)), sem((Z,)), sem((Z,)),
            sem((2 * Z,)), sem((2 * Z,)),
            sem((Z,)), sem((Z,)), sem((Z,)), sem((Z,)),
            sem((C,)), sem((C,)),
        ],
        compiler_params=pltpu.CompilerParams(
            collective_id=0, has_side_effects=True, vmem_limit_bytes=48 * 1024 * 1024
        ),
    )(tokens, gain[None, :], w_query, key_value_weight, cos, sin)


def solution(mesh):
    return jax.shard_map(
        lambda a, b, c, d: on_device(
            mesh.shape["seq"] // (2 * (d.shape[1] // (2 * HEAD_WIDTH))), a, b, c, d
        ),
        mesh=mesh,
        in_specs=(P(("grp", "seq"), None), P(), P("seq", None), P("seq", None)),
        out_specs=P(("grp", "seq"), None),
        check_vma=False,
    )
```

time: 389 us -> 112 us (0.29); the launches traced: 384 us -> 112 us
  waiting for transfers between devices: 258 us -> 0 us
  Pallas kernels: 0 us -> 108 us
  matrix products: 96.2 us -> 0 us
  between operations: 13.3 us -> 0.05 us
  other arithmetic: 12.9 us -> 1.01 us
    all_gather x3 -> x0, waiting for transfers between devices: 256 us -> none  [the longest x1 109 us: on_device(): query_raw = add_rows(lax.all_gather(w_query, 'seq', axis=0, tiled=True))]
    pallas_call x0 -> x1, Pallas kernels: none -> 108 us  [on_device(): pl.pallas_call(functools.partial(kernel, Z, C), out_shape=jax.ShapeDtypeS...]
    dot_general x66 -> x0, matrix products: 96.2 us -> none  [the longest x32 43.6 us: attend_block(): jnp.einsum('qhgk,khd->qhgd', expo.astype(jnp.bfloat16), kv_block[1], pref...]
    reduce_sum x33 -> x0, other arithmetic: 6.96 us -> none  [the longest x32 5.44 us: attend_block(): totals = totals * shrink + jnp.sum(expo, axis=-1)]
  transfers between devices with their start and end apart: 3 -> 0, of which waited for: 3 -> 0; matrix products, arithmetic and copies ran while one was open for 5% -> 0% of each run, Pallas kernels for 0% -> 0%
where the time goes in v1:
time: 112 us
  Pallas kernels  108 us (96%)
  local copies, waits for them, and re-layouts  2.98 us (3%)
    pallas_call x1, Pallas kernels, on_device(): pl.pallas_call(functools.partial(kernel, Z, C), out_shape=jax.ShapeDtypeS...  108 us
    unnamed x9, local copies, waits for them, and re-layouts  2.98 us

profile of v1, /device:TPU:27, one launch (start us, length us, event | category | flops | bytes accessed | tf_op | source)
XLA Modules:
  0.0 112.0 jit_solution(8499183360813773989)
XLA Ops:
  0.0 0.0 copy-start.1
  0.0 0.0 copy-start.3
  0.0 1.0 fusion
  1.0 0.0 copy-done.1
  1.0 0.0 copy-done.3
  1.1 0.0 copy-start
  1.1 1.2 %copy-done = bf16[128,4096]{1,0:T(8,128)(2,1)S(1)} copy-done((bf16[128,4096]{1,0:T(8,128)(2,1)S(1)}, bf16[128,4096]{1,0:T(8,128)(2,1)}, u32[]{:S(2)}) %copy-start) | copy-done | bytes 1048600
  2.3 0.0 copy-start.2
  2.3 0.9 copy-done.2
  3.2 108.0 %shard_map.46 = bf16[128,2048]{1,0:T(8,128)(2,1)S(1)} custom-call(bf16[128,4096]{1,0:T(8,128)(2,1)S(1)} %copy-done, f32[1,4096]{1,0:T(1,128)S(1)} %bitcast.1, bf16[128,2048]{1,0:T(8,128)(2,1)S(1)} %copy-done.1, bf16[128,1024]{1,0:T(8,128)(2,1)S(1)} %copy-done.2, f32[512,128]{1,0:T(8,128)S(1)} %get-tuple-element.6.cos_ref, ...), custom_call_target="tpu_custom_call" | custom-call | tf_op jit(solution)/shard_map/pallas_call | solution.py:335
  111.2 0.8 copy.6
  (2 shorter events, 0.0 us)
Async XLA Ops:
  0.0 1.0 copy-start.1
  0.0 1.0 copy-start.3
  1.1 1.2 %copy-start = (bf16[128,4096]{1,0:T(8,128)(2,1)S(1)}, bf16[128,4096]{1,0:T(8,128)(2,1)}, u32[]{:S(2)}) copy-start(bf16[128,4096]{1,0:T(8,128)(2,1)} %tok_ref.1) | copy-start | bytes 3145732
  2.3 0.9 copy-start.2

commit v2 on v1

v2 whole, which is shorter than its diff:
```python
import functools

import jax
import jax.numpy as jnp
from jax import lax
from jax.experimental import pallas as pl
from jax.experimental.pallas import tpu as pltpu
from jax.sharding import PartitionSpec as P

HEAD_WIDTH = 128
HQ = 16
ROPE_BASE = 500000.0
LOG2E = 1.4426950408889634
MESH = pl.DeviceIdType.MESH


def kernel(
    planes, kv_heads, tok_ref, gain_ref, wq_ref, wkv_ref, cos_ref, sin_ref, out_ref,
    kvst, qst, kvw, qw, xbuf, kacc, qacc, qbuf, kvbuf, mbuf, lbuf, obuf, ost, orecv,
    kw_s, kw_r, ku_s, ku_r, kd_s, kd_r, kb_s, kb_r,
    qw_s, qw_r, qu_s, qu_r, qd_s, qd_r, qb_s, qb_r,
    xs, xr, ks, kr, kss, ksr, os_, orr,
):
    C, Z, D = kv_heads, planes, HEAD_WIDTH
    T, M = tok_ref.shape
    G = HQ // C
    QW = G * D
    R = C * T
    me = lax.axis_index("seq")
    z = me // (2 * C)
    p = (me % (2 * C)) // 2
    k = me % 2

    def dev(zi, pi, ki):
        return {"seq": (zi * C + pi) * 2 + ki}

    sibling = dev(z, p, 1 - k)
    above = dev(lax.rem(z + 1, Z), p, k)
    below = dev(lax.rem(z + Z - 1, Z), p, k)
    has_above = z < Z - 1
    has_below = z > 0

    def copy(src, dst, send, recv, device):
        return pltpu.make_async_remote_copy(
            src_ref=src, dst_ref=dst, send_sem=send, recv_sem=recv,
            device_id=device, device_id_type=MESH,
        )

    def rows_of(owner):
        return pl.ds(pl.multiple_of(owner * T, T), T)

    barrier = pltpu.get_barrier_semaphore()
    for d in range(1, C):
        pl.semaphore_signal(barrier, inc=1, device_id=dev(z, lax.rem(p + d, C), k), device_id_type=MESH)
    pl.semaphore_signal(barrier, inc=1, device_id=sibling, device_id_type=MESH)

    @pl.when(has_above)
    def _():
        pl.semaphore_signal(barrier, inc=1, device_id=above, device_id_type=MESH)

    @pl.when(has_below)
    def _():
        pl.semaphore_signal(barrier, inc=1, device_id=below, device_id_type=MESH)

    kv_w = (kvst, kvw, kw_s, kw_r, ku_s, ku_r, kd_s, kd_r, kb_s, kb_r)
    q_w = (qst, qw, qw_s, qw_r, qu_s, qu_r, qd_s, qd_r, qb_s, qb_r)

    for c in range(C):
        kvst[c, :, :D] = wkv_ref[:, c * D:(c + 1) * D]
        kvst[c, :, D:] = wkv_ref[:, (C + c) * D:(C + c + 1) * D]
        qst[c] = wq_ref[:, c * QW:(c + 1) * QW]
    kvw[z, k, rows_of(p), :] = kvst[p]
    qw[z, k, rows_of(p), :] = qst[p]

    pl.semaphore_wait(barrier, C + has_above.astype(jnp.int32) + has_below.astype(jnp.int32))

    def plane_of(zi):
        return lax.rem(zi + Z, Z)

    def w_copy(w, d):
        to = lax.rem(p + d, C)
        return copy(w[0].at[to], w[1].at[z, k, rows_of(p), :], w[2].at[d], w[3].at[d], dev(z, to, k))

    def piece(w, d, s, device, ki=None, zi=None):
        frm = lax.rem(p + C - d, C)
        slot = w[1].at[z if zi is None else zi, k if ki is None else ki, rows_of(frm), :]
        return copy(slot, slot, w[s].at[d], w[s + 1].at[d], device)

    def block(w, zi, index, s, device, ki=None):
        slot = w[1].at[zi, k if ki is None else ki]
        return copy(slot, slot, w[s].at[C - 1 + index], w[s + 1].at[C - 1 + index], device)

    def send_piece(w, d):
        @pl.when(has_above)
        def _():
            piece(w, d, 4, above).start()

        @pl.when(has_below)
        def _():
            piece(w, d, 6, below).start()

        piece(w, d, 8, sibling).start()

    def first_step(w):
        for d in range(1, C):
            piece(w, d, 2, sibling).wait_recv()
            send_piece(w, d)

    def step(w, t):
        @pl.when(z >= t)
        def _():
            zi = plane_of(z - t)
            if t == 1:
                for d in range(C):
                    piece(w, d, 4, below, zi=zi).wait_recv()
            else:
                block(w, zi, t - 1, 4, below).wait_recv()

            @pl.when(has_above)
            def _():
                block(w, zi, t, 4, above).start()

            block(w, zi, t, 8, sibling).start()

        @pl.when(z + t < Z)
        def _():
            zi = plane_of(z + t)
            if t == 1:
                for d in range(C):
                    piece(w, d, 6, above, zi=zi).wait_recv()
            else:
                block(w, zi, t - 1, 6, above).wait_recv()

            @pl.when(has_below)
            def _():
                block(w, zi, t, 6, below).start()

            block(w, zi, Z - 1 + t, 8, sibling).start()

    def project(w, acc, zi):
        @pl.loop(0, R // 256)
        def _(i):
            rows = pl.ds(pl.multiple_of(i * 256, 256), 256)
            total = acc[rows, :]
            for ki in range(2):
                total += jnp.dot(
                    xbuf[zi * 2 + ki, rows, :], w[1][zi, ki],
                    preferred_element_type=jnp.float32,
                )
            acc[rows, :] = total

    def project_step(w, acc, t):
        if t == 0:
            for d in range(C):
                piece(w, d, 8, sibling, ki=1 - k).wait_recv()
            project(w, acc, z)
            return

        @pl.when(z >= t)
        def _():
            zi = plane_of(z - t)
            block(w, zi, t, 8, sibling, ki=1 - k).wait_recv()
            project(w, acc, zi)

        @pl.when(z + t < Z)
        def _():
            zi = plane_of(z + t)
            block(w, zi, Z - 1 + t, 8, sibling, ki=1 - k).wait_recv()
            project(w, acc, zi)

    def x_part(owner, half):
        return xbuf.at[:, pl.ds(pl.multiple_of(owner * T + half * (T // 2), T // 2), T // 2), :]

    peers = (p + 1 - 2 * lax.rem(p, 2), lax.rem(p + 2, 4))
    far = 3 - p

    def x_copy(peer, half, owner, index):
        part = x_part(owner, half)
        return copy(part, part, xs.at[index], xr.at[index], dev(z, peers[peer], k))

    def x_out(index):
        if index < 4:
            return x_copy(index // 2, index % 2, p, index)
        return x_copy(5 - index, index - 4, peers[index - 4], index)

    def x_in(index):
        if index < 4:
            return x_copy(index // 2, index % 2, peers[index // 2], index)
        return x_copy(5 - index, index - 4, far, index)

    for d in range(1, C):
        w_copy(kv_w, d).start()
    send_piece(kv_w, 0)
    for d in range(1, C):
        w_copy(q_w, d).start()
    send_piece(q_w, 0)

    @pl.loop(0, T // 16)
    def _(i):
        x = tok_ref[pl.ds(pl.multiple_of(i * 16, 16), 16), :].astype(jnp.float32)
        mean_sq = jnp.mean(x * x, axis=-1, keepdims=True)
        y = (x * lax.rsqrt(mean_sq + 1e-05) * gain_ref[...]).astype(jnp.bfloat16)
        rows = pl.ds(pl.multiple_of(p * T + i * 16, 16), 16)
        for zi in range(Z):
            for ki in range(2):
                for c in range(C):
                    j = ((zi * C + c) * 2 + ki) * T
                    xbuf[zi * 2 + ki, rows, c * T:(c + 1) * T] = y[:, j:j + T]

    for index in (0, 3, 1, 2):
        x_out(index).start()

    def forward_x():
        x_in(0).wait_recv()
        x_out(4).start()
        x_in(3).wait_recv()
        x_out(5).start()

    first_step(kv_w)
    first_step(q_w)
    kacc[...] = jnp.zeros_like(kacc)
    qacc[...] = jnp.zeros_like(qacc)
    for t in range(1, Z - 1):
        step(kv_w, t)
        step(q_w, t)
        if t == 1:
            forward_x()
    if Z < 3:
        forward_x()
    if Z > 1:
        step(kv_w, Z - 1)
    for index in (1, 2, 4, 5):
        x_in(index).wait_recv()
    for t in range(Z):
        project_step(kv_w, kacc, t)

    cos, sin = cos_ref[...], sin_ref[...]

    def rope(u):
        return (u * cos + pltpu.roll(u, D // 2, 1) * sin).astype(jnp.bfloat16)

    kvbuf[z, k, :, :D] = rope(kacc[:, :D])
    kvbuf[z, k, :, D:] = kacc[:, D:].astype(jnp.bfloat16)

    def block_copy(buf, zi, ki, send, recv, device):
        slot = buf.at[zi, ki]
        return copy(slot, slot, send, recv, device)

    def kv_up(t):
        return block_copy(kvbuf, plane_of(z - t), k, ks.at[t], kr.at[t], above)

    def kv_sib(t, ki):
        return block_copy(kvbuf, plane_of(z - t), ki, kss.at[t], ksr.at[t], sibling)

    kv_sib(0, k).start()

    @pl.when(has_above)
    def _():
        kv_up(0).start()

    def kv_recv(t):
        @pl.when(z >= t)
        def _():
            block_copy(kvbuf, plane_of(z - t), k, ks.at[t - 1], kr.at[t - 1], below).wait_recv()

            @pl.when(has_above)
            def _():
                kv_up(t).start()

            kv_sib(t, k).start()

    if Z > 1:
        kv_recv(1)
    for t in range(Z - 1):
        project_step(q_w, qacc, t)
    if Z > 1:
        step(q_w, Z - 1)
    if Z > 2:
        kv_recv(2)
    if Z > 1:
        project_step(q_w, qacc, Z - 1)
    else:
        project_step(q_w, qacc, 0)

    for h in range(G):
        qbuf[h] = rope(qacc[:, h * D:(h + 1) * D])

    factor = LOG2E / D**0.5
    half = R // 256

    def attend(zi, first):
        @pl.loop(0, G * half)
        def _(i):
            h = i // half
            r0 = pl.multiple_of((i % half) * 256, 256)
            rows = pl.ds(r0, 256)
            q = qbuf[h, rows, :]
            keys = kvbuf[zi, :, :, :D].reshape(2 * R, D)
            vals = kvbuf[zi, :, :, D:].reshape(2 * R, D)
            s = lax.dot_general(
                q, keys, (((1,), (1,)), ((), ())), preferred_element_type=jnp.float32
            )
            if first:
                row = r0 + lax.broadcasted_iota(jnp.int32, (256, 1), 0)
                col = lax.broadcasted_iota(jnp.int32, (1, 2 * R), 1)
                qpos = ((row // T) * 2 + k) * T + row % T
                kpos = (((col % R) // T) * 2 + col // R) * T + col % T
                s = jnp.where(kpos <= qpos, s, -1e30)
                m = jnp.max(s, axis=-1, keepdims=True)
            else:
                old = mbuf[h, rows, :1]
                m = jnp.maximum(old, jnp.max(s, axis=-1, keepdims=True))
            e = jnp.exp2((s - m) * factor)
            total = jnp.sum(e, axis=-1, keepdims=True)
            o = jnp.dot(e.astype(jnp.bfloat16), vals, preferred_element_type=jnp.float32)
            if not first:
                shrink = jnp.exp2((old - m) * factor)
                total += lbuf[h, rows, :1] * shrink
                o += obuf[h, rows, :] * shrink
            mbuf[h, rows, :] = jnp.broadcast_to(m, (256, D))
            lbuf[h, rows, :] = jnp.broadcast_to(total, (256, D))
            obuf[h, rows, :] = o

    kv_sib(0, 1 - k).wait_recv()
    attend(z, True)
    for t in range(1, Z):
        if t > 2:
            kv_recv(t)

        @pl.when(z >= t)
        def _():
            kv_sib(t, 1 - k).wait_recv()
            attend(plane_of(z - t), False)

    for c in range(C):
        for h in range(G):
            ost[c, :, h * D:(h + 1) * D] = (
                obuf[h, c * T:(c + 1) * T, :] / lbuf[h, c * T:(c + 1) * T, :]
            ).astype(jnp.bfloat16)

    def o_copy(d):
        to = lax.rem(p + d, C)
        return copy(ost.at[to], orecv.at[p], os_.at[d], orr.at[d], dev(z, to, k))

    for d in range(1, C):
        o_copy(d).start()
    orecv[p] = ost[p]
    for d in range(1, C):
        frm = lax.rem(p + C - d, C)
        copy(orecv.at[frm], orecv.at[frm], os_.at[d], orr.at[d], sibling).wait_recv()
    for c in range(C):
        out_ref[:, c * QW:(c + 1) * QW] = orecv[c]

    for d in range(1, C):
        o_copy(d).wait_send()
    for index in range(6):
        x_out(index).wait_send()
    for w in (kv_w, q_w):
        for d in range(C):
            if d > 0:
                w_copy(w, d).wait_send()

            @pl.when(has_above)
            def _():
                piece(w, d, 4, above).wait_send()

            @pl.when(has_below)
            def _():
                piece(w, d, 6, below).wait_send()

            piece(w, d, 8, sibling).wait_send()
        for t in range(1, Z):
            @pl.when(jnp.logical_and(has_above, z >= t))
            def _():
                block(w, plane_of(z - t), t, 4, above).wait_send()

            @pl.when(jnp.logical_and(has_below, z + t < Z))
            def _():
                block(w, plane_of(z + t), t, 6, below).wait_send()

            @pl.when(z >= t)
            def _():
                block(w, plane_of(z - t), t, 8, sibling).wait_send()

            @pl.when(z + t < Z)
            def _():
                block(w, plane_of(z + t), Z - 1 + t, 8, sibling).wait_send()
    for t in range(Z):
        @pl.when(jnp.logical_and(has_above, z >= t))
        def _():
            kv_up(t).wait_send()

        @pl.when(z >= t)
        def _():
            kv_sib(t, k).wait_send()


def on_device(planes, tokens, gain, w_query, key_value_weight):
    T, M = tokens.shape
    D = HEAD_WIDTH
    C = key_value_weight.shape[1] // (2 * D)
    G = HQ // C
    R = C * T
    Z = planes
    me = lax.axis_index("seq")
    first = (me // (2 * C)) * (2 * C) + me % 2
    row = jnp.arange(R, dtype=jnp.int32)
    positions = (first + (row // T) * 2) * T + row % T
    lane = jnp.arange(D, dtype=jnp.int32)
    half = (lane % (D // 2)).astype(jnp.float32)
    frequency = ROPE_BASE ** (-(half * 2.0 / D))
    angles = positions.astype(jnp.float32)[:, None] * frequency[None, :]
    cos = jnp.cos(angles)
    sin = jnp.where(lane < D // 2, -1.0, 1.0)[None, :] * jnp.sin(angles)
    bf, f32 = jnp.bfloat16, jnp.float32
    sem = pltpu.SemaphoreType.DMA
    vm = pl.BlockSpec(memory_space=pltpu.VMEM)
    return pl.pallas_call(
        functools.partial(kernel, Z, C),
        out_shape=jax.ShapeDtypeStruct((T, HQ * D), bf),
        in_specs=[vm] * 6,
        out_specs=vm,
        scratch_shapes=[
            pltpu.VMEM((C, T, 2 * D), bf),
            pltpu.VMEM((C, T, G * D), bf),
            pltpu.VMEM((Z, 2, R, 2 * D), bf),
            pltpu.VMEM((Z, 2, R, G * D), bf),
            pltpu.VMEM((2 * Z, R, M // (2 * Z)), bf),
            pltpu.VMEM((R, 2 * D), f32),
            pltpu.VMEM((R, G * D), f32),
            pltpu.VMEM((G, R, D), bf),
            pltpu.VMEM((Z, 2, R, 2 * D), bf),
            pltpu.VMEM((G, R, D), f32),
            pltpu.VMEM((G, R, D), f32),
            pltpu.VMEM((G, R, D), f32),
            pltpu.VMEM((C, T, G * D), bf),
            pltpu.VMEM((C, T, G * D), bf),
            sem((C,)), sem((C,)), sem((C + Z,)), sem((C + Z,)),
            sem((C + Z,)), sem((C + Z,)), sem((C + 2 * Z,)), sem((C + 2 * Z,)),
            sem((C,)), sem((C,)), sem((C + Z,)), sem((C + Z,)),
            sem((C + Z,)), sem((C + Z,)), sem((C + 2 * Z,)), sem((C + 2 * Z,)),
            sem((6,)), sem((6,)),
            sem((Z,)), sem((Z,)), sem((Z,)), sem((Z,)),
            sem((C,)), sem((C,)),
        ],
        compiler_params=pltpu.CompilerParams(
            collective_id=0, has_side_effects=True, vmem_limit_bytes=48 * 1024 * 1024
        ),
    )(tokens, gain[None, :], w_query, key_value_weight, cos, sin)


def solution(mesh):
    return jax.shard_map(
        lambda a, b, c, d: on_device(
            mesh.shape["seq"] // (2 * (d.shape[1] // (2 * HEAD_WIDTH))), a, b, c, d
        ),
        mesh=mesh,
        in_specs=(P(("grp", "seq"), None), P(), P("seq", None), P("seq", None)),
        out_specs=P(("grp", "seq"), None),
        check_vma=False,
    )
```

time: 112 us -> 107 us (0.955)
  Pallas kernels: 108 us -> 102 us
    pallas_call x1, Pallas kernels: 108 us -> 102 us  [on_device(): pl.pallas_call(functools.partial(kernel, Z, C), out_shape=jax.ShapeDtypeS...]
where the time goes in v2:
time: 107 us; the launch traced here: 106 us
  Pallas kernels  102 us (95%)
  local copies, waits for them, and re-layouts  2.98 us (3%)
    pallas_call x1, Pallas kernels, on_device(): pl.pallas_call(functools.partial(kernel, Z, C), out_shape=jax.ShapeDtypeS...  102 us
    unnamed x9, local copies, waits for them, and re-layouts  2.98 us

profile of v2, /device:TPU:27, one launch (start us, length us, event | category | flops | bytes accessed | tf_op | source)
XLA Modules:
  0.0 106.1 jit_solution(7893224795860579156)
XLA Ops:
  0.0 0.0 copy-start.1
  0.0 0.0 copy-start.3
  0.0 1.0 fusion
  1.0 0.0 copy-done.1
  1.0 0.0 copy-done.3
  1.1 0.0 copy-start
  1.1 1.2 %copy-done = bf16[128,4096]{1,0:T(8,128)(2,1)S(1)} copy-done((bf16[128,4096]{1,0:T(8,128)(2,1)S(1)}, bf16[128,4096]{1,0:T(8,128)(2,1)}, u32[]{:S(2)}) %copy-start) | copy-done | bytes 1048600
  2.3 0.0 copy-start.2
  2.3 0.9 copy-done.2
  3.2 102.1 %shard_map.46 = bf16[128,2048]{1,0:T(8,128)(2,1)S(1)} custom-call(bf16[128,4096]{1,0:T(8,128)(2,1)S(1)} %copy-done, f32[1,4096]{1,0:T(1,128)S(1)} %bitcast.1, bf16[128,2048]{1,0:T(8,128)(2,1)S(1)} %copy-done.1, bf16[128,1024]{1,0:T(8,128)(2,1)S(1)} %copy-done.2, f32[512,128]{1,0:T(8,128)S(1)} %get-tuple-element.6.cos_ref, ...), custom_call_target="tpu_custom_call" | custom-call | tf_op jit(solution)/shard_map/pallas_call | solution.py:418
  105.3 0.8 copy.6
  (2 shorter events, 0.0 us)
Async XLA Ops:
  0.0 1.0 copy-start.1
  0.0 1.0 copy-start.3
  1.1 1.2 %copy-start = (bf16[128,4096]{1,0:T(8,128)(2,1)S(1)}, bf16[128,4096]{1,0:T(8,128)(2,1)}, u32[]{:S(2)}) copy-start(bf16[128,4096]{1,0:T(8,128)(2,1)} %tok_ref.1) | copy-start | bytes 3145732
  2.3 0.9 copy-start.2
